TPU v7x, 512 devices: a whole 4x8x8 slice. The times are simulated.
512 devices in a mesh: lon: 64 (over x, z_lo, y), lat: 8 (over z_hi, core).
Axes of the slice: x: 4, y: 8, z: 8 (z_hi: 4, z_lo: 2; z = z_hi * 2 + z_lo), core: 2. Of those that a mesh axis runs over, the one named last changes fastest.
Arguments:
- temp: float32 [75, 16, 8192], P(None, 'lat', 'lon'), may hold values from -6 to 6
- salt: float32 [75, 16, 8192], P(None, 'lat', 'lon'), may hold values from -6 to 6
- uvel: float32 [75, 16, 8192], P(None, 'lat', 'lon'), may hold values from -0.4 to 0.4
- vvel: float32 [75, 16, 8192], P(None, 'lat', 'lon'), may hold values from -0.4 to 0.4
- land_mask: int32 [16, 8192], P('lat', 'lon'), may hold values 0 or 1
- bottom: int32 [16, 8192], P('lat', 'lon'), may hold values from 1 to 75
Outputs:
- temp_out: float32 [75, 16, 8192], P(None, 'lat', 'lon')
- salt_out: float32 [75, 16, 8192], P(None, 'lat', 'lon')
- uvel_out: float32 [75, 16, 8192], P(None, 'lat', 'lon')
- vvel_out: float32 [75, 16, 8192], P(None, 'lat', 'lon')
All inputs are finite; a program needn't handle non-finite values. No bound on the sum of `land_mask` on one device may be relied on, other than what follows from the above.
Results may differ from a plain program's by a relative error of at most 0.0003.
Values sent between devices are 32-bit elements; how exact they have to be, the bound alone decides.
No kernel may reach another device: no remote copies, remote signals or barrier semaphores. Data moves between devices by JAX's collectives and lax.ppermute only.
A program may use at most 64 MiB of HBM per device.

v0:
```python
import jax
import jax.numpy as jnp
from jax import lax
from jax.sharding import PartitionSpec as P

alpha_surface = 0.3
alpha_depth = 0.004
alpha_square = 0.05
beta_salt = 0.7
thermo_salt = 0.03
press_scale = 0.02
coriolis_base = 0.08
coriolis_slope = 0.06
mixing_base = 0.3
mixing_convect = 3.0
mixing_sharp = 3.0


def padded_2(block, sides, width, periodic):
    for axis, dim in sides:
        count = lax.axis_size(axis)
        forward = [(i, i + 1) for i in range(count - 1)]
        if periodic:
            forward.append((count - 1, 0))
        backward = [(target, source) for source, target in forward]
        low = lax.ppermute(
            lax.slice_in_dim(block, block.shape[dim] - width, None, axis=dim), axis, forward
        )
        high = lax.ppermute(lax.slice_in_dim(block, 0, width, axis=dim), axis, backward)
        block = jnp.concatenate([low, block, high], axis=dim)
    return block


def swapped(shard, axis, bit):
    return lax.ppermute(shard, axis, [(i, i ^ 1 << bit) for i in range(lax.axis_size(axis))])


def density(temp_field, salt_field, depth_index):
    return (
        -(alpha_surface + alpha_depth * depth_index) * temp_field
        - alpha_square * temp_field * temp_field
        + beta_salt * salt_field
        - thermo_salt * temp_field * salt_field
    )


def fold_sign(levels):
    return jnp.concatenate(
        [
            jnp.ones((2 * levels,), jnp.float32),
            -jnp.ones((2 * levels,), jnp.float32),
            jnp.ones((1,), jnp.float32),
        ]
    )


def face_fluxes(upwind_far, upwind_near, downwind_near, downwind_far, face_speed, opening):
    centred = (
        face_speed * (7.0 * (upwind_near + downwind_near) - (upwind_far + downwind_far)) / 12.0
    )
    damping = (
        jnp.abs(face_speed)
        * (3.0 * (downwind_near - upwind_near) - (downwind_far - upwind_far))
        / 12.0
    )
    return opening * (centred - damping)


def advect_field(field, zonal_speed, merid_speed, wet):
    row_count = field.shape[-2] - 4
    col_count = field.shape[-1] - 4
    band_rows = field[..., 2 : row_count + 2, :]
    speed_rows = zonal_speed[:, 2 : row_count + 2, :]
    wet_rows = wet[:, 2 : row_count + 2, :]
    face_speed = 0.5 * (speed_rows[..., 1 : col_count + 2] + speed_rows[..., 2 : col_count + 3])
    opening = wet_rows[..., 1 : col_count + 2] * wet_rows[..., 2 : col_count + 3]
    zonal_fluxes = face_fluxes(
        band_rows[..., 0 : col_count + 1],
        band_rows[..., 1 : col_count + 2],
        band_rows[..., 2 : col_count + 3],
        band_rows[..., 3 : col_count + 4],
        face_speed,
        opening,
    )
    zonal_part = -(zonal_fluxes[..., 1:] - zonal_fluxes[..., :-1])
    band_cols = field[..., :, 2 : col_count + 2]
    speed_cols = merid_speed[:, :, 2 : col_count + 2]
    wet_cols = wet[:, :, 2 : col_count + 2]
    face_speed = 0.5 * (
        speed_cols[..., 1 : row_count + 2, :] + speed_cols[..., 2 : row_count + 3, :]
    )
    opening = wet_cols[..., 1 : row_count + 2, :] * wet_cols[..., 2 : row_count + 3, :]
    merid_fluxes = face_fluxes(
        band_cols[..., 0 : row_count + 1, :],
        band_cols[..., 1 : row_count + 2, :],
        band_cols[..., 2 : row_count + 3, :],
        band_cols[..., 3 : row_count + 4, :],
        face_speed,
        opening,
    )
    merid_part = -(merid_fluxes[..., 1:, :] - merid_fluxes[..., :-1, :])
    return zonal_part + merid_part


def vertical_solve(kappa, rhs):
    levels = rhs.shape[1]
    nothing = jnp.zeros_like(kappa[0])
    uppers = []
    values = []
    for layer_index in range(levels):
        above_coef = kappa[layer_index - 1] if layer_index > 0 else nothing
        below_coef = kappa[layer_index] if layer_index < levels - 1 else nothing
        diagonal_coef = 1.0 + above_coef + below_coef
        if layer_index == 0:
            pivot_value = diagonal_coef
            solved_value = rhs[:, 0] / pivot_value
        else:
            pivot_value = diagonal_coef + above_coef * uppers[-1]
            solved_value = (rhs[:, layer_index] + above_coef * values[-1]) / pivot_value
        uppers.append(-below_coef / pivot_value)
        values.append(solved_value)
    result = [values[-1]]
    for layer_index in range(levels - 2, -1, -1):
        result.append(values[layer_index] - uppers[layer_index] * result[-1])
    return jnp.stack(result[::-1], axis=1)


def finish(fields, wet, pressure, tendency, depth_index, first_row, lat_total):
    row_count = fields.shape[2] - 4
    inner = wet[:, 2:-2, 2:-2]
    centre = fields[:, :, 2:-2, 2:-2]
    grad_x = (
        0.5
        * (pressure[:, 2:-2, 3:-1] - pressure[:, 2:-2, 1:-3])
        * wet[:, 2:-2, 3:-1]
        * wet[:, 2:-2, 1:-3]
    )
    grad_y = (
        0.5
        * (pressure[:, 3:-1, 2:-2] - pressure[:, 1:-3, 2:-2])
        * wet[:, 3:-1, 2:-2]
        * wet[:, 1:-3, 2:-2]
    )
    rows_global = (first_row + jnp.arange(row_count, dtype=jnp.int32)).astype(jnp.float32)
    spin = (coriolis_base + coriolis_slope * rows_global / lat_total)[:, None]
    temp_star = centre[0] + inner * tendency[0]
    salt_star = centre[1] + inner * tendency[1]
    east_star = centre[2] + inner * (tendency[2] + spin * centre[3] - grad_x)
    north_star = centre[3] + inner * (tendency[3] - spin * centre[2] - grad_y)
    rho_star = density(temp_star, salt_star, depth_index)
    kappa = (
        (
            mixing_base
            + mixing_convect * jax.nn.sigmoid(mixing_sharp * (rho_star[:-1] - rho_star[1:]))
        )
        * inner[:-1]
        * inner[1:]
    )
    rhs = jnp.stack([temp_star, salt_star, east_star, north_star])
    return vertical_solve(kappa, rhs)


def shards(temp, salt, uvel, vvel, land_mask, bottom):
    levels, row_count, col_count = temp.shape
    depth = (land_mask * bottom).astype(jnp.float32)
    stack = jnp.concatenate([temp, salt, uvel, vvel, depth[None]], axis=0)
    padded = padded_2(stack, (("lat", 1),), 2, False)
    partner = stack
    for bit_index in range(lax.axis_size("lon").bit_length() - 1):
        partner = swapped(partner, "lon", bit_index)
    mirrored = partner[:, ::-1, ::-1] * fold_sign(levels)[:, None, None]
    on_top = lax.axis_index("lat") == lax.axis_size("lat") - 1
    upper_ghost = jnp.where(on_top, mirrored, padded[:, row_count + 2 :, :])
    padded = jnp.concatenate([padded[:, : row_count + 2, :], upper_ghost], axis=1)
    full = padded_2(padded, (("lon", 2),), 2, True)
    fields = full[: 4 * levels].reshape(4, levels, row_count + 4, col_count + 4)
    depth_index = jnp.arange(levels, dtype=jnp.float32)[:, None, None]
    wet = (depth_index < full[4 * levels][None]).astype(jnp.float32)
    rho = density(fields[0], fields[1], depth_index)
    lower_ones = (jnp.arange(levels)[:, None] >= jnp.arange(levels)[None, :]).astype(jnp.float32)
    pressure = press_scale * jnp.dot(
        lower_ones, rho.reshape(levels, -1), precision=lax.Precision.HIGHEST
    ).reshape(rho.shape)
    tendency = advect_field(fields, fields[2], fields[3], wet)
    first_row = lax.axis_index("lat") * row_count
    result = finish(
        fields, wet, pressure, tendency, depth_index, first_row, row_count * lax.axis_size("lat")
    )
    return (result[0], result[1], result[2], result[3])


def solution(mesh):
    placed = (
        P(None, "lat", "lon"),
        P(None, "lat", "lon"),
        P(None, "lat", "lon"),
        P(None, "lat", "lon"),
        P("lat", "lon"),
        P("lat", "lon"),
    )
    return jax.shard_map(
        shards,
        mesh=mesh,
        in_specs=placed,
        out_specs=(
            P(None, "lat", "lon"),
            P(None, "lat", "lon"),
            P(None, "lat", "lon"),
            P(None, "lat", "lon"),
        ),
        check_vma=False,
    )
```

profile of v0, /device:TPU:1, one launch (start us, length us, event | category | flops | bytes accessed | tf_op | source)
XLA Modules:
  0.0 182.0 jit_solution(8978414336655124403)
XLA Ops:
  5.5 4.0 %collective-permute-start.1 = (f32[301,2,128]{2,0,1:T(8,128)S(1)}, f32[301,2,128]{2,0,1:T(8,128)S(1)}, u32[]{:S(2)}, u32[]{:S(2)}) collective-permute-start(f32[301,2,128]{2,0,1:T(8,128)S(1)} %concatenate.21), channel_id=1, source_target_pairs={{0,8},{8,0},{16,24},{24,16},{32,40},{40,32},{48,56},{56,48},{64,72... | collective-permute-start | bytes 924680 | tf_op jit(solution)/shard_map/ppermute | solution.py:35
  9.6 4.3 %collective-permute-done.1 = f32[301,2,128]{2,0,1:T(8,128)S(1)} collective-permute-done((f32[301,2,128]{2,0,1:T(8,128)S(1)}, f32[301,2,128]{2,0,1:T(8,128)S(1)}, u32[]{:S(2)}, u32[]{:S(2)}) %collective-permute-start.1) | collective-permute-done | bytes 308256 | tf_op jit(solution)/shard_map/ppermute | solution.py:35
  13.9 6.8 %collective-permute-start.2 = (f32[301,2,128]{2,0,1:T(8,128)S(1)}, f32[301,2,128]{2,0,1:T(8,128)S(1)}, u32[]{:S(2)}, u32[]{:S(2)}) collective-permute-start(f32[301,2,128]{2,0,1:T(8,128)S(1)} %collective-permute-done.1), channel_id=1, source_target_pairs={{0,16},{8,24},{16,0},{24,8},{32,48},{40,56},{48,32},{56,40},{64,80... | collective-permute-start | bytes 924680 | tf_op jit(solution)/shard_map/ppermute | solution.py:35
  20.7 13.2 %collective-permute-done.2 = f32[301,2,128]{2,0,1:T(8,128)S(1)} collective-permute-done((f32[301,2,128]{2,0,1:T(8,128)S(1)}, f32[301,2,128]{2,0,1:T(8,128)S(1)}, u32[]{:S(2)}, u32[]{:S(2)}) %collective-permute-start.2) | collective-permute-done | bytes 308256 | tf_op jit(solution)/shard_map/ppermute | solution.py:35
  33.9 8.7 %collective-permute-start.3 = (f32[301,2,128]{2,0,1:T(8,128)S(1)}, f32[301,2,128]{2,0,1:T(8,128)S(1)}, u32[]{:S(2)}, u32[]{:S(2)}) collective-permute-start(f32[301,2,128]{2,0,1:T(8,128)S(1)} %collective-permute-done.2), channel_id=1, source_target_pairs={{0,32},{8,40},{16,48},{24,56},{32,0},{40,8},{48,16},{56,24},{64,96... | collective-permute-start | bytes 924680 | tf_op jit(solution)/shard_map/ppermute | solution.py:35
  42.6 13.0 %collective-permute-done.3 = f32[301,2,128]{2,0,1:T(8,128)S(1)} collective-permute-done((f32[301,2,128]{2,0,1:T(8,128)S(1)}, f32[301,2,128]{2,0,1:T(8,128)S(1)}, u32[]{:S(2)}, u32[]{:S(2)}) %collective-permute-start.3) | collective-permute-done | bytes 308256 | tf_op jit(solution)/shard_map/ppermute | solution.py:35
  55.6 3.9 %collective-permute-start.4 = (f32[301,2,128]{2,0,1:T(8,128)S(1)}, f32[301,2,128]{2,0,1:T(8,128)S(1)}, u32[]{:S(2)}, u32[]{:S(2)}) collective-permute-start(f32[301,2,128]{2,0,1:T(8,128)S(1)} %collective-permute-done.3), channel_id=1, source_target_pairs={{0,64},{8,72},{16,80},{24,88},{32,96},{40,104},{48,112},{56,120},{... | collective-permute-start | bytes 924680 | tf_op jit(solution)/shard_map/ppermute | solution.py:35
  59.6 6.3 %collective-permute-done.4 = f32[301,2,128]{2,0,1:T(8,128)S(1)} collective-permute-done((f32[301,2,128]{2,0,1:T(8,128)S(1)}, f32[301,2,128]{2,0,1:T(8,128)S(1)}, u32[]{:S(2)}, u32[]{:S(2)}) %collective-permute-start.4) | collective-permute-done | bytes 308256 | tf_op jit(solution)/shard_map/ppermute | solution.py:35
  65.9 3.1 %collective-permute-start.5 = (f32[301,2,128]{2,0,1:T(8,128)S(1)}, f32[301,2,128]{2,0,1:T(8,128)S(1)}, u32[]{:S(2)}, u32[]{:S(2)}) collective-permute-start(f32[301,2,128]{2,0,1:T(8,128)S(1)} %collective-permute-done.4), channel_id=1, source_target_pairs={{0,128},{8,136},{16,144},{24,152},{32,160},{40,168},{48,176},{56,1... | collective-permute-start | bytes 924680 | tf_op jit(solution)/shard_map/ppermute | solution.py:35
  69.0 5.7 %collective-permute-done.5 = f32[301,2,128]{2,0,1:T(8,128)S(1)} collective-permute-done((f32[301,2,128]{2,0,1:T(8,128)S(1)}, f32[301,2,128]{2,0,1:T(8,128)S(1)}, u32[]{:S(2)}, u32[]{:S(2)}) %collective-permute-start.5) | collective-permute-done | bytes 308256 | tf_op jit(solution)/shard_map/ppermute | solution.py:35
  74.7 4.6 %collective-permute-start.6 = (f32[301,2,128]{2,0,1:T(8,128)S(1)}, f32[301,2,128]{2,0,1:T(8,128)S(1)}, u32[]{:S(2)}, u32[]{:S(2)}) collective-permute-start(f32[301,2,128]{2,0,1:T(8,128)S(1)} %collective-permute-done.5), channel_id=1, source_target_pairs={{0,256},{8,264},{16,272},{24,280},{32,288},{40,296},{48,304},{56,3... | collective-permute-start | bytes 924680 | tf_op jit(solution)/shard_map/ppermute | solution.py:35
  79.3 5.1 %collective-permute-start.7 = (f32[301,2,128]{2,0,1:T(8,128)S(1)}, f32[301,2,128]{2,0,1:T(8,128)S(1)}, u32[]{:S(2)}, u32[]{:S(2)}) collective-permute-start(f32[301,2,128]{2,0,1:T(8,128)S(1)} %concatenate.21), channel_id=1, source_target_pairs={{1,0},{2,1},{3,2},{4,3},{5,4},{6,5},{7,6},{9,8},{10,9},{11,10},{12... | collective-permute-start | bytes 924680 | tf_op jit(solution)/shard_map/ppermute | solution.py:29
  84.4 5.7 %collective-permute-start = (f32[301,2,128]{2,0,1:T(8,128)S(1)}, f32[301,2,128]{2,0,1:T(8,128)S(1)}, u32[]{:S(2)}, u32[]{:S(2)}) collective-permute-start(f32[301,2,128]{2,0,1:T(8,128)S(1)} %concatenate.21), channel_id=1, source_target_pairs={{0,1},{1,2},{2,3},{3,4},{4,5},{5,6},{6,7},{8,9},{9,10},{10,11},{11... | collective-permute-start | bytes 924680 | tf_op jit(solution)/shard_map/ppermute | solution.py:26
  91.5 4.6 %collective-permute-done.7 = f32[301,2,128]{2,0,1:T(8,128)S(1)} collective-permute-done((f32[301,2,128]{2,0,1:T(8,128)S(1)}, f32[301,2,128]{2,0,1:T(8,128)S(1)}, u32[]{:S(2)}, u32[]{:S(2)}) %collective-permute-start.7) | collective-permute-done | bytes 308256 | tf_op jit(solution)/shard_map/ppermute | solution.py:29
  97.6 8.7 %collective-permute-start.9 = (f32[301,6,2]{0,1,2:T(8,128)S(1)}, f32[301,6,2]{0,1,2:T(8,128)S(1)}, u32[]{:S(2)}, u32[]{:S(2)}) collective-permute-start(f32[301,6,2]{0,1,2:T(8,128)S(1)} %copy.7247), channel_id=1, source_target_pairs={{8,0},{16,8},{24,16},{32,24},{40,32},{48,40},{56,48},{64,56},{72,6... | collective-permute-start | bytes 43352 | tf_op jit(solution)/shard_map/ppermute | solution.py:29
  106.3 1.9 %collective-permute-start.8 = (f32[301,6,2]{0,1,2:T(8,128)S(1)}, f32[301,6,2]{0,1,2:T(8,128)S(1)}, u32[]{:S(2)}, u32[]{:S(2)}) collective-permute-start(f32[301,6,2]{0,1,2:T(8,128)S(1)} %copy.7246), channel_id=1, source_target_pairs={{0,8},{8,16},{16,24},{24,32},{32,40},{40,48},{48,56},{56,64},{64,7... | collective-permute-start | bytes 43352 | tf_op jit(solution)/shard_map/ppermute | solution.py:26
  109.9 5.2 %collective-permute-done.8 = f32[301,6,2]{0,1,2:T(8,128)S(1)} collective-permute-done((f32[301,6,2]{0,1,2:T(8,128)S(1)}, f32[301,6,2]{0,1,2:T(8,128)S(1)}, u32[]{:S(2)}, u32[]{:S(2)}) %collective-permute-start.8) | collective-permute-done | bytes 14480 | tf_op jit(solution)/shard_map/ppermute | solution.py:26
  118.8 1.7 copy.7255
  120.5 1.7 copy.7254
  122.3 2.0 %pad_maximum_fusion = f32[301,6,132]{2,0,1:T(8,128)} fusion(f32[301,6,2]{2,0,1:T(8,128)S(1)} %copy.7249, f32[301,2,128]{2,0,1:T(8,128)S(1)} %multiply_select_fusion, f32[301,2,128]{2,0,1:T(8,128)S(1)} %concatenate.21, f32[301,2,128]{2,0,1:T(8,128)S(1)} %collective-permute-done, f32[301,6,2]{2,0,1:T(8,128)S(1)} %copy.7248), kind=kLoop, calls=%fused_computation | loop fusion | flops 953568 | bytes 1907136 | tf_op jit(solution)/shard_map/concatenate | solution.py:30
  124.3 3.2 %copy.7250 = f32[300,6,132]{0,2,1:T(8,128)} copy(f32[300,6,132]{2,0,1:T(8,128)} %bitcast.1288) | data formatting | bytes 1900800 | tf_op jit(solution)/shard_map/slice | solution.py:176
  127.5 2.5 %reshape.109 = f32[4,75,6,132]{1,0,3,2:T(4,128)S(1)} reshape(f32[300,6,132]{0,2,1:T(8,128)} %copy.7250) | data formatting | bytes 1900800 | tf_op jit(solution)/shard_map/reshape | solution.py:176
  131.2 1.6 copy.7263
  132.8 1.6 copy.7260
  134.5 1.7 copy.7256
  136.2 1.7 copy.7251
  141.8 1.6 copy.7262
  143.5 1.6 copy.7259
  145.1 1.9 %fusion.13 = (f32[75,2,128]{2,1,0:T(2,128)S(1)}, f32[75,2,128]{2,1,0:T(2,128)}, f32[75,2,128]{2,1,0:T(2,128)}) fusion(f32[75]{0:T(128)S(1)} %add_negate_fusion, f32[75,2,128]{2,1,0:T(2,128)} %copy.7260, f32[75,2,128]{2,1,0:T(2,128)} %copy.7259, f32[75,6,132]{2,1,0:T(8,128)S(1)} %copy-done.7, f32[75,2,128]{2,1,0:T(2,128)} %copy.7263, f32[75,2,128]{2,1,0:T(2,128)} %copy.7262), kind=kLoop, calls=%fused_computation.112 | loop fusion | flops 249600 | bytes 614700 | tf_op jit(solution)/shard_map/sub | solution.py:40
  152.5 1.9 %fusion.6 = f32[75,6,132]{2,0,1:T(8,128)} fusion(f32[301,6,2]{2,0,1:T(8,128)S(1)} %copy.7249, f32[301,2,128]{2,0,1:T(8,128)S(1)} %copy-done.3, f32[301,2,128]{2,0,1:T(8,128)S(1)} %copy-done.1, f32[301,2,128]{2,0,1:T(8,128)S(1)} %copy-done.5, f32[301,6,2]{2,0,1:T(8,128)S(1)} %copy.7248, f32[75]{0:T(128)} %copy-done.73), kind=kLoop, calls=%fused_computation.14 | loop fusion | flops 1009800 | bytes 1191468 | tf_op jit(solution)/shard_map/sub | solution.py:40
  159.7 2.4 %fusion.103 = (f32[4,1,2,128]{3,2,0,1:T(2,128)S(1)}, f32[4,2,128]{2,1,0:T(2,128)S(1)}, f32[4,2,128]{2,1,0:T(2,128)S(1)}, f32[4,2,128]{2,1,0:T(2,128)S(1)}, f32[4...) fusion(f32[2,128]{1,0:T(2,128)S(1)} %copy-done.26, ...), kind=kLoop, calls=%fused_computation.619 | loop fusion | flops 230400 | bytes 665600 | tf_op jit(solution)/shard_map/stack | solution.py:125
  177.5 2.7 %constant_dynamic-update-slice_fusion.62 = (f32[4,75,2,128]{3,0,2,1:T(4,128)S(1)}, f32[4,1,2,128]{3,0,2,1:T(4,128)S(1)}, f32[4,1,2,128]{3,0,2,1:T(4,128)S(1)}, f...) fusion(f32[4,75,2,128]{3,0,2,1:T(4,128)S(1)} %constant_dynamic-, ...), kind=kLoop, calls=%fused_computation.90 | loop fusion | flops 355328 | bytes 650240
  (300 shorter events, 44.8 us)
Async XLA Ops:
  0.6 95.5 %copy-start.72 = (f32[301]{0:T(512)S(1)}, f32[301]{0:T(512)}, u32[]{:S(2)}) copy-start(f32[301]{0:T(512)} %constant.19.clone.1) | copy-start | bytes 3616
  5.5 116.7 %copy-start = (f32[301,2,128]{2,0,1:T(8,128)}, f32[301,2,128]{2,0,1:T(8,128)S(1)}, u32[]{:S(2)}) copy-start(f32[301,2,128]{2,0,1:T(8,128)S(1)} %concatenate.21) | copy-start | bytes 924676
  5.5 8.3 %collective-permute-start.1 = (f32[301,2,128]{2,0,1:T(8,128)S(1)}, f32[301,2,128]{2,0,1:T(8,128)S(1)}, u32[]{:S(2)}, u32[]{:S(2)}) collective-permute-start(f32[301,2,128]{2,0,1:T(8,128)S(1)} %concatenate.21), channel_id=1, source_target_pairs={{0,8},{8,0},{16,24},{24,16},{32,40},{40,32},{48,56},{56,48},{64,72... | collective-permute-start | bytes 924680 | tf_op jit(solution)/shard_map/ppermute | solution.py:35
  13.9 20.0 %collective-permute-start.2 = (f32[301,2,128]{2,0,1:T(8,128)S(1)}, f32[301,2,128]{2,0,1:T(8,128)S(1)}, u32[]{:S(2)}, u32[]{:S(2)}) collective-permute-start(f32[301,2,128]{2,0,1:T(8,128)S(1)} %collective-permute-done.1), channel_id=1, source_target_pairs={{0,16},{8,24},{16,0},{24,8},{32,48},{40,56},{48,32},{56,40},{64,80... | collective-permute-start | bytes 924680 | tf_op jit(solution)/shard_map/ppermute | solution.py:35
  33.9 21.7 %collective-permute-start.3 = (f32[301,2,128]{2,0,1:T(8,128)S(1)}, f32[301,2,128]{2,0,1:T(8,128)S(1)}, u32[]{:S(2)}, u32[]{:S(2)}) collective-permute-start(f32[301,2,128]{2,0,1:T(8,128)S(1)} %collective-permute-done.2), channel_id=1, source_target_pairs={{0,32},{8,40},{16,48},{24,56},{32,0},{40,8},{48,16},{56,24},{64,96... | collective-permute-start | bytes 924680 | tf_op jit(solution)/shard_map/ppermute | solution.py:35
  55.6 10.3 %collective-permute-start.4 = (f32[301,2,128]{2,0,1:T(8,128)S(1)}, f32[301,2,128]{2,0,1:T(8,128)S(1)}, u32[]{:S(2)}, u32[]{:S(2)}) collective-permute-start(f32[301,2,128]{2,0,1:T(8,128)S(1)} %collective-permute-done.3), channel_id=1, source_target_pairs={{0,64},{8,72},{16,80},{24,88},{32,96},{40,104},{48,112},{56,120},{... | collective-permute-start | bytes 924680 | tf_op jit(solution)/shard_map/ppermute | solution.py:35
  65.9 8.8 %collective-permute-start.5 = (f32[301,2,128]{2,0,1:T(8,128)S(1)}, f32[301,2,128]{2,0,1:T(8,128)S(1)}, u32[]{:S(2)}, u32[]{:S(2)}) collective-permute-start(f32[301,2,128]{2,0,1:T(8,128)S(1)} %collective-permute-done.4), channel_id=1, source_target_pairs={{0,128},{8,136},{16,144},{24,152},{32,160},{40,168},{48,176},{56,1... | collective-permute-start | bytes 924680 | tf_op jit(solution)/shard_map/ppermute | solution.py:35
  74.7 16.0 %collective-permute-start.6 = (f32[301,2,128]{2,0,1:T(8,128)S(1)}, f32[301,2,128]{2,0,1:T(8,128)S(1)}, u32[]{:S(2)}, u32[]{:S(2)}) collective-permute-start(f32[301,2,128]{2,0,1:T(8,128)S(1)} %collective-permute-done.5), channel_id=1, source_target_pairs={{0,256},{8,264},{16,272},{24,280},{32,288},{40,296},{48,304},{56,3... | collective-permute-start | bytes 924680 | tf_op jit(solution)/shard_map/ppermute | solution.py:35
  79.3 16.8 %collective-permute-start.7 = (f32[301,2,128]{2,0,1:T(8,128)S(1)}, f32[301,2,128]{2,0,1:T(8,128)S(1)}, u32[]{:S(2)}, u32[]{:S(2)}) collective-permute-start(f32[301,2,128]{2,0,1:T(8,128)S(1)} %concatenate.21), channel_id=1, source_target_pairs={{1,0},{2,1},{3,2},{4,3},{5,4},{6,5},{7,6},{9,8},{10,9},{11,10},{12... | collective-permute-start | bytes 924680 | tf_op jit(solution)/shard_map/ppermute | solution.py:29
  84.4 11.8 %collective-permute-start = (f32[301,2,128]{2,0,1:T(8,128)S(1)}, f32[301,2,128]{2,0,1:T(8,128)S(1)}, u32[]{:S(2)}, u32[]{:S(2)}) collective-permute-start(f32[301,2,128]{2,0,1:T(8,128)S(1)} %concatenate.21), channel_id=1, source_target_pairs={{0,1},{1,2},{2,3},{3,4},{4,5},{5,6},{6,7},{8,9},{9,10},{10,11},{11... | collective-permute-start | bytes 924680 | tf_op jit(solution)/shard_map/ppermute | solution.py:26
  90.1 55.0 %copy-start.73 = (f32[75]{0:T(128)}, f32[75]{0:T(128)S(1)}, u32[]{:S(2)}) copy-start(f32[75]{0:T(128)S(1)} %add_negate_fusion) | copy-start | bytes 904
  96.2 26.1 %copy-start.2 = (f32[301,2,128]{2,0,1:T(8,128)}, f32[301,2,128]{2,0,1:T(8,128)S(1)}, u32[]{:S(2)}) copy-start(f32[301,2,128]{2,0,1:T(8,128)S(1)} %multiply_select_fusion) | copy-start | bytes 924676
  96.2 26.0 %copy-start.4 = (f32[301,2,128]{2,0,1:T(8,128)}, f32[301,2,128]{2,0,1:T(8,128)S(1)}, u32[]{:S(2)}) copy-start(f32[301,2,128]{2,0,1:T(8,128)S(1)} %collective-permute-done) | copy-start | bytes 924676
  97.6 17.9 %collective-permute-start.9 = (f32[301,6,2]{0,1,2:T(8,128)S(1)}, f32[301,6,2]{0,1,2:T(8,128)S(1)}, u32[]{:S(2)}, u32[]{:S(2)}) collective-permute-start(f32[301,6,2]{0,1,2:T(8,128)S(1)} %copy.7247), channel_id=1, source_target_pairs={{8,0},{16,8},{24,16},{32,24},{40,32},{48,40},{56,48},{64,56},{72,6... | collective-permute-start | bytes 43352 | tf_op jit(solution)/shard_map/ppermute | solution.py:29
  106.3 8.8 %collective-permute-start.8 = (f32[301,6,2]{0,1,2:T(8,128)S(1)}, f32[301,6,2]{0,1,2:T(8,128)S(1)}, u32[]{:S(2)}, u32[]{:S(2)}) collective-permute-start(f32[301,6,2]{0,1,2:T(8,128)S(1)} %copy.7246), channel_id=1, source_target_pairs={{0,8},{8,16},{16,24},{24,32},{32,40},{40,48},{48,56},{56,64},{64,7... | collective-permute-start | bytes 43352 | tf_op jit(solution)/shard_map/ppermute | solution.py:26
  159.2 18.2 %copy-start.55 = (f32[2,128]{1,0:T(2,128)S(1)}, f32[2,128]{1,0:T(2,128)}, u32[]{:S(2)}) copy-start(f32[2,128]{1,0:T(2,128)} %get-tuple-element.276) | copy-start | bytes 3076
  159.2 18.2 %copy-start.56 = (f32[2,128]{1,0:T(2,128)S(1)}, f32[2,128]{1,0:T(2,128)}, u32[]{:S(2)}) copy-start(f32[2,128]{1,0:T(2,128)} %get-tuple-element.280) | copy-start | bytes 3076
  162.1 18.1 %copy-start.71 = (f32[1,2,128]{2,1,0:T(2,128)S(1)}, f32[1,2,128]{2,1,0:T(2,128)}, u32[]{:S(2)}) copy-start(f32[1,2,128]{2,1,0:T(2,128)} %get-tuple-element.384) | copy-start | bytes 3076
  162.1 18.1 %copy-start.70 = (f32[1,2,128]{2,1,0:T(2,128)S(1)}, f32[1,2,128]{2,1,0:T(2,128)}, u32[]{:S(2)}) copy-start(f32[1,2,128]{2,1,0:T(2,128)} %get-tuple-element.380) | copy-start | bytes 3076
  162.1 18.2 %copy-start.69 = (f32[1,2,128]{2,1,0:T(2,128)S(1)}, f32[1,2,128]{2,1,0:T(2,128)}, u32[]{:S(2)}) copy-start(f32[1,2,128]{2,1,0:T(2,128)} %get-tuple-element.376) | copy-start | bytes 3076
  162.1 18.2 %copy-start.68 = (f32[1,2,128]{2,1,0:T(2,128)S(1)}, f32[1,2,128]{2,1,0:T(2,128)}, u32[]{:S(2)}) copy-start(f32[1,2,128]{2,1,0:T(2,128)} %get-tuple-element.372) | copy-start | bytes 3076
  162.1 18.2 %copy-start.67 = (f32[1,2,128]{2,1,0:T(2,128)S(1)}, f32[1,2,128]{2,1,0:T(2,128)}, u32[]{:S(2)}) copy-start(f32[1,2,128]{2,1,0:T(2,128)} %get-tuple-element.368) | copy-start | bytes 3076
  162.1 18.2 %copy-start.66 = (f32[1,2,128]{2,1,0:T(2,128)S(1)}, f32[1,2,128]{2,1,0:T(2,128)}, u32[]{:S(2)}) copy-start(f32[1,2,128]{2,1,0:T(2,128)} %get-tuple-element.364) | copy-start | bytes 3076
  162.1 18.3 %copy-start.65 = (f32[1,2,128]{2,1,0:T(2,128)S(1)}, f32[1,2,128]{2,1,0:T(2,128)}, u32[]{:S(2)}) copy-start(f32[1,2,128]{2,1,0:T(2,128)} %get-tuple-element.360) | copy-start | bytes 3076
  162.1 18.3 %copy-start.64 = (f32[1,2,128]{2,1,0:T(2,128)S(1)}, f32[1,2,128]{2,1,0:T(2,128)}, u32[]{:S(2)}) copy-start(f32[1,2,128]{2,1,0:T(2,128)} %get-tuple-element.356) | copy-start | bytes 3076
  162.1 18.3 %copy-start.63 = (f32[1,2,128]{2,1,0:T(2,128)S(1)}, f32[1,2,128]{2,1,0:T(2,128)}, u32[]{:S(2)}) copy-start(f32[1,2,128]{2,1,0:T(2,128)} %get-tuple-element.352) | copy-start | bytes 3076
  162.1 18.4 %copy-start.62 = (f32[1,2,128]{2,1,0:T(2,128)S(1)}, f32[1,2,128]{2,1,0:T(2,128)}, u32[]{:S(2)}) copy-start(f32[1,2,128]{2,1,0:T(2,128)} %get-tuple-element.348) | copy-start | bytes 3076
  162.2 18.4 %copy-start.61 = (f32[1,2,128]{2,1,0:T(2,128)S(1)}, f32[1,2,128]{2,1,0:T(2,128)}, u32[]{:S(2)}) copy-start(f32[1,2,128]{2,1,0:T(2,128)} %get-tuple-element.344) | copy-start | bytes 3076
  162.2 18.4 %copy-start.60 = (f32[1,2,128]{2,1,0:T(2,128)S(1)}, f32[1,2,128]{2,1,0:T(2,128)}, u32[]{:S(2)}) copy-start(f32[1,2,128]{2,1,0:T(2,128)} %get-tuple-element.340) | copy-start | bytes 3076
  162.2 18.4 %copy-start.59 = (f32[1,2,128]{2,1,0:T(2,128)S(1)}, f32[1,2,128]{2,1,0:T(2,128)}, u32[]{:S(2)}) copy-start(f32[1,2,128]{2,1,0:T(2,128)} %get-tuple-element.336) | copy-start | bytes 3076
  162.2 18.5 %copy-start.58 = (f32[1,2,128]{2,1,0:T(2,128)S(1)}, f32[1,2,128]{2,1,0:T(2,128)}, u32[]{:S(2)}) copy-start(f32[1,2,128]{2,1,0:T(2,128)} %get-tuple-element.332) | copy-start | bytes 3076
  162.2 18.5 %copy-start.57 = (f32[1,2,128]{2,1,0:T(2,128)S(1)}, f32[1,2,128]{2,1,0:T(2,128)}, u32[]{:S(2)}) copy-start(f32[1,2,128]{2,1,0:T(2,128)} %get-tuple-element.328) | copy-start | bytes 3076
  (52 other events, 174.5 us)
where the time goes:
time: 183 us; the launch traced here: 182 us
  starting transfers between devices  52.7 us (29%)
  waiting for transfers between devices  52.2 us (29%)
  other arithmetic  39.1 us (21%)
  local copies, waits for them, and re-layouts  35.4 us (19%)
  between operations  2.32 us (1%)
    ppermute x6, waiting for transfers between devices, swapped(): lax.ppermute(shard, axis, [(i, i ^ 1 << bit) for i in range(lax.axis_size...  42.5 us
    ppermute x6, starting transfers between devices, swapped(): lax.ppermute(shard, axis, [(i, i ^ 1 << bit) for i in range(lax.axis_size...  31.2 us
    another operation x22, other arithmetic, vertical_solve(): return jnp.stack(result[::-1], axis=1)  17.4 us
    ppermute x2, starting transfers between devices, padded_2(): lax.ppermute(lax.slice_in_dim(block, 0, width, axis=dim), axis, backward)  13.8 us
    ppermute x2, starting transfers between devices, padded_2(): lax.ppermute(lax.slice_in_dim(block, block.shape[dim] - width, None, axis...  7.63 us
    ppermute x2, waiting for transfers between devices, padded_2(): lax.ppermute(lax.slice_in_dim(block, block.shape[dim] - width, None, axis...  5.18 us
    ppermute x2, waiting for transfers between devices, padded_2(): lax.ppermute(lax.slice_in_dim(block, 0, width, axis=dim), axis, backward)  4.59 us
    unnamed x211, local copies, waits for them, and re-layouts  4.4 us
  transfers between devices with their start and end apart: 10, of which 7 were waited for; matrix products, arithmetic and copies ran while one was open for 2% of the time, Pallas kernels for 0%

commit v1 on v0

v1 whole, which is shorter than its diff:
```python
import functools

import jax
import jax.numpy as jnp
from jax import lax
from jax.experimental import pallas as pl
from jax.experimental.pallas import tpu as pltpu
from jax.sharding import PartitionSpec as P

alpha_surface = 0.3
alpha_depth = 0.004
alpha_square = 0.05
beta_salt = 0.7
thermo_salt = 0.03
press_scale = 0.02
coriolis_base = 0.08
coriolis_slope = 0.06
mixing_base = 0.3
mixing_convect = 3.0
mixing_sharp = 3.0

LANES = 128
ROWS = 2
FIELDS = 4
VMEM_LIMIT = 24 * 1024 * 1024


class Sizes:
    def __init__(self, levels):
        self.levels = levels
        self.used = levels * ROWS
        self.chunks = -(-self.used // 8)
        self.padded = self.chunks * 8
        self.depth_at = FIELDS * self.padded
        self.total = self.depth_at + 8
        self.col_slots = -(-self.chunks // 4)


def iotas():
    lane = lax.broadcasted_iota(jnp.int32, (8, LANES), 1)
    row = lax.broadcasted_iota(jnp.int32, (8, LANES), 0)
    return lane, row


def pack_kernel(
    sz, temp, salt, uvel, vvel, mask, bottom, rows, cols, mask_v, bottom_v, sems
):
    copies = []
    for f, field in enumerate((temp, salt, uvel, vvel)):
        copy = pltpu.make_async_copy(
            field.reshape(sz.used, LANES),
            rows.at[pl.ds(f * sz.padded, sz.used)],
            sems.at[f],
        )
        copy.start()
        copies.append(copy)
    planes = []
    for i, (source, target) in enumerate(((mask, mask_v), (bottom, bottom_v))):
        copy = pltpu.make_async_copy(source, target, sems.at[FIELDS + i])
        copy.start()
        planes.append(copy)
    lane, row = iotas()
    for copy in planes:
        copy.wait()
    depth = (mask_v[...] * bottom_v[...]).astype(jnp.float32)
    pattern = jnp.where(row % 2 == 0, depth[0:1], depth[1:2])
    rows[sz.depth_at : sz.total, :] = pattern
    for copy in copies:
        copy.wait()
    if sz.padded > sz.used:
        for f in range(FIELDS):
            rows[f * sz.padded + sz.used : (f + 1) * sz.padded, :] = jnp.zeros(
                (sz.padded - sz.used, LANES), jnp.float32
            )
    place = lane // 4
    for s in range(sz.col_slots):
        packed = jnp.zeros((8, LANES), jnp.float32)
        for g in range(4):
            chunk = 4 * s + g
            if chunk < sz.chunks:
                for f in range(FIELDS):
                    part = rows[f * sz.padded + 8 * chunk : f * sz.padded + 8 * chunk + 8, :]
                    part = pltpu.roll(part, 32 * g + 4 * f + 2, 1)
                    packed = jnp.where(place == 8 * g + f, part, packed)
        packed = jnp.where(place == 4, pltpu.roll(pattern, 18, 1), packed)
        cols[8 * s : 8 * s + 8, :] = packed


def step_kernel(
    sz, own, pair_a, pair_b, col_e, col_w, out_t, out_s, out_u, out_v,
    south, north, star, coef, value, gain, outs, sems,
):
    levels = sz.levels
    lon = lax.axis_index("lon")
    lat = lax.axis_index("lat")
    lat_count = lax.axis_size("lat")
    lane, row = iotas()
    even_row = row % 2 == 0
    odd_lat = lat % 2 == 1
    on_top = lat == lat_count - 1

    def swap_rows(x):
        return jnp.where(even_row, pltpu.roll(x, 7, 0), pltpu.roll(x, 1, 0))

    def fill(ref, source):
        for at in range(0, sz.total, 8):
            ref[at : at + 8, :] = source[at : at + 8, :]

    @pl.when(odd_lat)
    def _():
        fill(south, pair_a)

    @pl.when(jnp.logical_not(odd_lat))
    def _():
        fill(south, pair_b)
        fill(north, pair_a)

    @pl.when(odd_lat & jnp.logical_not(on_top))
    def _():
        fill(north, pair_b)

    @pl.when(on_top)
    def _():
        back = LANES - 1 - lane
        for at in range(0, sz.total, 8):
            x = swap_rows(pair_b[at : at + 8, :])
            x = jnp.take_along_axis(x, back, axis=1)
            if 2 * sz.padded <= at < sz.depth_at:
                x = -x
            north[at : at + 8, :] = x

    even_lon = lon % 2 == 0
    from_east = lane % 4 >= 2
    pick = from_east == even_lon
    halo = [
        jnp.where(pick, col_e[8 * s : 8 * s + 8, :], col_w[8 * s : 8 * s + 8, :])
        for s in range(sz.col_slots)
    ]

    def lon_shift(x, h, by):
        if by > 0:
            return pltpu.roll(jnp.where(lane < by, h, x), LANES - by, 1)
        return pltpu.roll(jnp.where(lane >= LANES + by, h, x), -by, 1)

    def row_north(x, g):
        return jnp.where(even_row, pltpu.roll(x, 7, 0), pltpu.roll(g, 1, 0))

    def row_south(x, g):
        return jnp.where(even_row, pltpu.roll(g, 7, 0), pltpu.roll(x, 1, 0))

    def density(t, s, lin):
        return beta_salt * s - t * (lin + alpha_square * t + thermo_salt * s)

    depth = own[sz.depth_at : sz.total, :]
    depth_h = pltpu.roll(halo[0], LANES - 18, 1)
    depth_e = lon_shift(depth, depth_h, 1)
    depth_w = lon_shift(depth, depth_h, -1)
    depth_n = row_north(depth, north[sz.depth_at : sz.total, :])
    depth_s = row_south(depth, south[sz.depth_at : sz.total, :])
    low_e, low_w = jnp.minimum(depth, depth_e), jnp.minimum(depth, depth_w)
    low_n, low_s = jnp.minimum(depth, depth_n), jnp.minimum(depth, depth_s)
    low_x, low_y = jnp.minimum(low_e, low_w), jnp.minimum(low_n, low_s)

    spin_row = (lat * ROWS + row % 2).astype(jnp.float32)
    spin = coriolis_base + coriolis_slope * spin_row / (ROWS * lat_count)
    zero = jnp.zeros((8, LANES), jnp.float32)
    level_in = (row // 2).astype(jnp.float32)

    sum_x, sum_y, rho_before = zero, zero, zero
    for v in range(sz.chunks):
        def load(ref, f):
            return ref[f * sz.padded + 8 * v : f * sz.padded + 8 * v + 8, :]

        level = level_in + 4.0 * v
        c = [load(own, f) for f in range(FIELDS)]
        g_n = [load(north, f) for f in range(FIELDS)]
        g_s = [load(south, f) for f in range(FIELDS)]
        slot, group = v // 4, v % 4
        h = [
            pltpu.roll(halo[slot], LANES - (32 * group + 4 * f + 2), 1) for f in range(FIELDS)
        ]
        e1 = [lon_shift(c[f], h[f], 1) for f in range(FIELDS)]
        e2 = [lon_shift(c[f], h[f], 2) for f in range(FIELDS)]
        w1 = [lon_shift(c[f], h[f], -1) for f in range(FIELDS)]
        w2 = [lon_shift(c[f], h[f], -2) for f in range(FIELDS)]
        n1 = [row_north(c[f], g_n[f]) for f in range(FIELDS)]
        s1 = [row_south(c[f], g_s[f]) for f in range(FIELDS)]

        def faces(speed_lo, speed_mid, speed_hi, low_lo, low_hi):
            up = jnp.where(level < low_hi, (speed_mid + speed_hi) * (1.0 / 24.0), 0.0)
            dn = jnp.where(level < low_lo, (speed_lo + speed_mid) * (1.0 / 24.0), 0.0)
            a_up, a_dn = jnp.abs(up), jnp.abs(dn)
            p_up, q_up = up + a_up, up - a_up
            p_dn, q_dn = dn + a_dn, dn - a_dn
            near_up, far_up = 5.0 * p_up + 2.0 * q_up, 2.0 * p_up + 5.0 * q_up
            near_dn, far_dn = 5.0 * p_dn + 2.0 * q_dn, 2.0 * p_dn + 5.0 * q_dn
            return -p_dn, near_dn + p_up, far_dn - near_up, -(far_up + q_dn), q_up

        z = faces(w1[2], c[2], e1[2], low_w, low_e)
        m = faces(s1[3], c[3], n1[3], low_s, low_n)
        mid = z[2] + m[2]
        adv = [
            (z[0] * w2[f] + z[1] * w1[f])
            + (z[3] * e1[f] + z[4] * e2[f])
            + (m[0] * g_s[f] + m[1] * s1[f])
            + (m[3] * n1[f] + m[4] * g_n[f])
            + mid * c[f]
            for f in range(FIELDS)
        ]

        lin = alpha_surface + alpha_depth * level
        scale = 0.5 * press_scale
        d_x = scale * (density(e1[0], e1[1], lin) - density(w1[0], w1[1], lin))
        d_y = scale * (density(n1[0], n1[1], lin) - density(s1[0], s1[1], lin))

        def prefix(d, total):
            part = d + jnp.where(row >= 2, pltpu.roll(d, 2, 0), 0.0)
            part = part + jnp.where(row >= 4, pltpu.roll(part, 4, 0), 0.0)
            both = d + pltpu.roll(d, 4, 0)
            return total + part, total + (both + pltpu.roll(both, 2, 0))

        p_x, sum_x = prefix(d_x, sum_x)
        p_y, sum_y = prefix(d_y, sum_y)
        wet = level < depth
        grad_x = jnp.where(level < low_x, p_x, 0.0)
        grad_y = jnp.where(level < low_y, p_y, 0.0)
        turn = jnp.where(wet, spin, 0.0)
        new = [
            c[0] + adv[0],
            c[1] + adv[1],
            c[2] + (adv[2] + turn * c[3] - grad_x),
            c[3] + (adv[3] - turn * c[2] - grad_y),
        ]
        rho = density(new[0], new[1], lin)
        above = jnp.where(row < 2, pltpu.roll(rho_before, 2, 0), pltpu.roll(rho, 2, 0))
        rho_before = rho
        mix = (mixing_base + 0.5 * mixing_convect) + (0.5 * mixing_convect) * jnp.tanh(
            (0.5 * mixing_sharp) * (above - rho)
        )
        open_above = wet if v else wet & (row >= 2)
        a = jnp.where(open_above, mix, 0.0)

        for i, x in enumerate(exchange(new, row)):
            star[8 * (4 * v + i) : 8 * (4 * v + i) + 8, :] = x
        for i, x in enumerate(spread(a, row)):
            coef[8 * (4 * v + i) : 8 * (4 * v + i) + 8, :] = x

    def at(ref, k):
        return ref[8 * k : 8 * k + 8, :]

    middle = (levels + 1) // 2
    one = jnp.ones((8, LANES), jnp.float32)
    a_next = at(coef, 0)
    theta, phi, y = one, zero, zero
    theta_b, phi_b, y_b = one, zero, zero
    b_next = zero
    for i in range(middle):
        k = i
        a_k, a_next = a_next, at(coef, k + 1)
        phi = theta + a_k * phi
        theta_new = phi + a_next * theta
        inverse = theta * pl.reciprocal(theta_new, approx=False)
        y = inverse * (at(star, k) + a_k * y)
        value[8 * k : 8 * k + 8, :] = y
        gain[8 * k : 8 * k + 8, :] = a_next * inverse
        theta = theta_new
        k = levels - 1 - i
        if k >= middle:
            b_k, b_next = b_next, at(coef, k)
            phi_b = theta_b + b_k * phi_b
            theta_new = phi_b + b_next * theta_b
            inverse = theta_b * pl.reciprocal(theta_new, approx=False)
            y_b = inverse * (at(star, k) + b_k * y_b)
            value[8 * k : 8 * k + 8, :] = y_b
            gain[8 * k : 8 * k + 8, :] = b_next * inverse
            theta_b = theta_new

    alpha, beta = at(gain, middle - 1), at(gain, middle)
    x_up = (y + alpha * y_b) * pl.reciprocal(1.0 - alpha * beta, approx=False)
    x_dn = y_b + beta * x_up
    value[8 * (middle - 1) : 8 * middle, :] = x_up
    value[8 * middle : 8 * middle + 8, :] = x_dn
    for i in range(1, middle):
        k = middle - 1 - i
        x_up = at(value, k) + at(gain, k) * x_up
        value[8 * k : 8 * k + 8, :] = x_up
        k = middle + i
        if k < levels:
            x_dn = at(value, k) + at(gain, k) * x_dn
            value[8 * k : 8 * k + 8, :] = x_dn

    for v in range(sz.chunks):
        group = [at(value, 4 * v + i) if 4 * v + i < levels else zero for i in range(4)]
        for f, x in enumerate(exchange(group, row)):
            outs[f, 8 * v : 8 * v + 8, :] = x
    copies = []
    for f, ref in enumerate((out_t, out_s, out_u, out_v)):
        copy = pltpu.make_async_copy(
            outs.at[f, pl.ds(0, sz.used)], ref.reshape(sz.used, LANES), sems.at[f]
        )
        copy.start()
        copies.append(copy)
    for copy in copies:
        copy.wait()


def exchange(x, row):
    upper = row < 4
    half = [
        jnp.where(upper, x[0], pltpu.roll(x[2], 4, 0)),
        jnp.where(upper, x[1], pltpu.roll(x[3], 4, 0)),
        jnp.where(upper, pltpu.roll(x[0], 4, 0), x[2]),
        jnp.where(upper, pltpu.roll(x[1], 4, 0), x[3]),
    ]
    first = row % 4 < 2
    return [
        jnp.where(first, half[0], pltpu.roll(half[1], 2, 0)),
        jnp.where(first, pltpu.roll(half[0], 6, 0), half[1]),
        jnp.where(first, half[2], pltpu.roll(half[3], 2, 0)),
        jnp.where(first, pltpu.roll(half[2], 6, 0), half[3]),
    ]


def spread(x, row):
    upper, first = row < 4, row % 4 < 2
    turned = pltpu.roll(x, 4, 0)
    low, high = jnp.where(upper, x, turned), jnp.where(upper, turned, x)
    low_t, high_t = pltpu.roll(low, 2, 0), pltpu.roll(high, 2, 0)
    return [
        jnp.where(first, low, low_t),
        jnp.where(first, low_t, low),
        jnp.where(first, high, high_t),
        jnp.where(first, high_t, high),
    ]


def partners(names, sizes):
    lon_count, lat_count = sizes["lon"], sizes["lat"]

    def flat(lon, lat):
        at = {"lon": lon, "lat": lat}
        index = 0
        for name in names:
            index = index * sizes[name] + at[name]
        return index

    everyone = [(lon, lat) for lon in range(lon_count) for lat in range(lat_count)]
    pair_a = [(flat(i, j), flat(i, j ^ 1)) for i, j in everyone]
    pair_b = []
    for i, j in everyone:
        if j == lat_count - 1:
            pair_b.append((flat(i, j), flat(lon_count - 1 - i, j)))
        elif j > 0:
            pair_b.append((flat(i, j), flat(i, j + 1 if j % 2 else j - 1)))
    lon_1 = [(flat(i, j), flat(i ^ 1, j)) for i, j in everyone]
    lon_2 = [
        (flat(i, j), flat((i + 1 if i % 2 else i - 1) % lon_count, j)) for i, j in everyone
    ]
    return pair_a, pair_b, lon_1, lon_2


def shards(names, sizes, temp, salt, uvel, vvel, land_mask, bottom):
    sz = Sizes(temp.shape[0])
    hbm = pl.BlockSpec(memory_space=pltpu.HBM)
    vmem = pl.BlockSpec(memory_space=pltpu.VMEM)
    f32 = jnp.float32
    rows, cols = pl.pallas_call(
        functools.partial(pack_kernel, sz),
        out_shape=(
            pltpu.VMEM((sz.total, LANES), f32),
            pltpu.VMEM((8 * sz.col_slots, LANES), f32),
        ),
        in_specs=[hbm] * 6,
        out_specs=(vmem, vmem),
        scratch_shapes=[
            pltpu.VMEM(land_mask.shape, jnp.int32),
            pltpu.VMEM(land_mask.shape, jnp.int32),
            pltpu.SemaphoreType.DMA((FIELDS + 2,)),
        ],
        name="pack",
    )(temp, salt, uvel, vvel, land_mask, bottom)
    pair_a, pair_b, lon_1, lon_2 = partners(names, sizes)
    from_b = lax.ppermute(rows, names, pair_b)
    from_1 = lax.ppermute(cols, names, lon_1)
    from_2 = lax.ppermute(cols, names, lon_2)
    from_a = lax.ppermute(rows, names, pair_a)
    field = jax.ShapeDtypeStruct(temp.shape, f32)
    tall = 8 * 4 * sz.chunks
    return pl.pallas_call(
        functools.partial(step_kernel, sz),
        out_shape=(field,) * 4,
        in_specs=[vmem] * 5,
        out_specs=(hbm,) * 4,
        scratch_shapes=[
            pltpu.VMEM((sz.total, LANES), f32),
            pltpu.VMEM((sz.total, LANES), f32),
            pltpu.VMEM((tall, LANES), f32),
            pltpu.VMEM((tall, LANES), f32),
            pltpu.VMEM((tall, LANES), f32),
            pltpu.VMEM((tall, LANES), f32),
            pltpu.VMEM((FIELDS, sz.padded, LANES), f32),
            pltpu.SemaphoreType.DMA((FIELDS,)),
        ],
        compiler_params=pltpu.CompilerParams(vmem_limit_bytes=VMEM_LIMIT),
        name="step",
    )(rows, from_a, from_b, from_1, from_2)


def solution(mesh):
    names = tuple(mesh.axis_names)
    sizes = dict(mesh.shape)
    field = P(None, "lat", "lon")
    plane = P("lat", "lon")
    return jax.shard_map(
        functools.partial(shards, names, sizes),
        mesh=mesh,
        in_specs=(field,) * 4 + (plane,) * 2,
        out_specs=(field,) * 4,
        check_vma=False,
    )
```

time: 183 us -> 27.5 us (0.15)
  the two profiles are of different devices: /device:TPU:1 before, /device:TPU:128 now
where the time goes in v1:
time: 27.5 us; the launch traced here: 27.3 us
  starting transfers between devices  19.7 us (72%)
  waiting for transfers between devices  3.75 us (14%)
  Pallas kernels  3.12 us (11%)
  between operations  0.68 us (2%)
    ppermute x1, starting transfers between devices, shards(): from_2 = lax.ppermute(cols, names, lon_2)  8.48 us
    ppermute x1, starting transfers between devices, shards(): from_a = lax.ppermute(rows, names, pair_a)  7.4 us
    ppermute x1, waiting for transfers between devices, shards(): from_1 = lax.ppermute(cols, names, lon_1)  3.74 us
    ppermute x1, starting transfers between devices, shards(): from_b = lax.ppermute(rows, names, pair_b)  1.92 us
    ppermute x1, starting transfers between devices, shards(): from_1 = lax.ppermute(cols, names, lon_1)  1.92 us
    pallas_call x1, Pallas kernels, shards(): pl.pallas_call(functools.partial(step_kernel, sz), out_shape=(field,) * 4...  1.92 us
    pallas_call x1, Pallas kernels, shards(): pl.pallas_call(functools.partial(pack_kernel, sz), out_shape=(pltpu.VMEM(...  1.2 us
  transfers between devices with their start and end apart: 4, of which 1 were waited for; matrix products, arithmetic and copies ran while one was open for 0% of the time, Pallas kernels for 0%

profile of v1, /device:TPU:128, one launch (start us, length us, event | category | flops | bytes accessed | tf_op | source)
XLA Modules:
  0.0 27.3 jit_solution(16630618358151258214)
XLA Ops:
  0.6 1.2 %pack.1 = (f32[616,128]{1,0:T(8,128)S(1)}, f32[40,128]{1,0:T(8,128)S(1)}) custom-call(f32[75,2,128]{2,1,0:T(2,128)} %temp.1, f32[75,2,128]{2,1,0:T(2,128)} %salt.1, f32[75,2,128]{2,1,0:T(2,128)} %uvel.1, f32[75,2,128]{2,1,0:T(2,128)} %vvel.1, s32[2,128]{1,0:T(2,128)} %mask.1, s32[2,128]{1,0:T(2,128)} %bottom.1), custom_call_target="tpu_custom_call" | custom-call | tf_op jit(solution)/shard_map/pack/pallas_call | solution.py:367
  1.8 1.9 %collective-permute-start.1 = (f32[616,128]{1,0:T(8,128)S(1)}, f32[616,128]{1,0:T(8,128)S(1)}, u32[]{:S(2)}, u32[]{:S(2)}) collective-permute-start(f32[616,128]{1,0:T(8,128)S(1)} %get-tuple-element.6.own), channel_id=1, source_target_pairs={{1,2},{2,1},{3,4},{4,3},{5,6},{6,5},{7,511},{9,10},{10,9},{11,12},... | collective-permute-start | bytes 946184 | tf_op jit(solution)/shard_map/ppermute | solution.py:383
  3.8 7.4 %collective-permute-start = (f32[616,128]{1,0:T(8,128)S(1)}, f32[616,128]{1,0:T(8,128)S(1)}, u32[]{:S(2)}, u32[]{:S(2)}) collective-permute-start(f32[616,128]{1,0:T(8,128)S(1)} %get-tuple-element.6.own), channel_id=1, source_target_pairs={{0,1},{1,0},{2,3},{3,2},{4,5},{5,4},{6,7},{7,6},{8,9},{9,8},{10,11... | collective-permute-start | bytes 946184 | tf_op jit(solution)/shard_map/ppermute | solution.py:386
  11.2 8.5 %collective-permute-start.3 = (f32[40,128]{1,0:T(8,128)S(1)}, f32[40,128]{1,0:T(8,128)S(1)}, u32[]{:S(2)}, u32[]{:S(2)}) collective-permute-start(f32[40,128]{1,0:T(8,128)S(1)} %get-tuple-element.7), channel_id=1, source_target_pairs={{0,504},{1,505},{2,506},{3,507},{4,508},{5,509},{6,510},{7,511},{8... | collective-permute-start | bytes 61448 | tf_op jit(solution)/shard_map/ppermute | solution.py:385
  19.7 1.9 %collective-permute-start.2 = (f32[40,128]{1,0:T(8,128)S(1)}, f32[40,128]{1,0:T(8,128)S(1)}, u32[]{:S(2)}, u32[]{:S(2)}) collective-permute-start(f32[40,128]{1,0:T(8,128)S(1)} %get-tuple-element.7), channel_id=1, source_target_pairs={{0,8},{1,9},{2,10},{3,11},{4,12},{5,13},{6,14},{7,15},{8,0},{9,1},... | collective-permute-start | bytes 61448 | tf_op jit(solution)/shard_map/ppermute | solution.py:384
  21.6 0.0 collective-permute-done.3.col_w
  21.6 3.7 %collective-permute-done.2.col_e = f32[40,128]{1,0:T(8,128)S(1)} collective-permute-done((f32[40,128]{1,0:T(8,128)S(1)}, f32[40,128]{1,0:T(8,128)S(1)}, u32[]{:S(2)}, u32[]{:S(2)}) %collective-permute-start.2) | collective-permute-done | bytes 20512 | tf_op jit(solution)/shard_map/ppermute | solution.py:384
  25.3 0.0 collective-permute-done.1.pair_b
  25.3 0.0 collective-permute-done.pair_a
  25.4 1.9 %step.1 = (f32[75,2,128]{2,1,0:T(2,128)}, f32[75,2,128]{2,1,0:T(2,128)}, f32[75,2,128]{2,1,0:T(2,128)}, f32[75,2,128]{2,1,0:T(2,128)}) custom-call(f32[616,128]{1,0:T(8,128)S(1)} %get-tuple-element.6.own, f32[616,128]{1,0:T(8,128)S(1)} %collective-permute-done.pair_a, f32[616,128]{1,0:T(8,128)S(1)} %collective-permute-done.1.pair_b, ...), custom_call_target="tpu_custom_call" | custom-call | tf_op jit(solution)/shard_map/step/pallas_call | solution.py:389
Async XLA Ops:
  1.8 23.5 %collective-permute-start.1 = (f32[616,128]{1,0:T(8,128)S(1)}, f32[616,128]{1,0:T(8,128)S(1)}, u32[]{:S(2)}, u32[]{:S(2)}) collective-permute-start(f32[616,128]{1,0:T(8,128)S(1)} %get-tuple-element.6.own), channel_id=1, source_target_pairs={{1,2},{2,1},{3,4},{4,3},{5,6},{6,5},{7,511},{9,10},{10,9},{11,12},... | collective-permute-start | bytes 946184 | tf_op jit(solution)/shard_map/ppermute | solution.py:383
  3.8 21.6 %collective-permute-start = (f32[616,128]{1,0:T(8,128)S(1)}, f32[616,128]{1,0:T(8,128)S(1)}, u32[]{:S(2)}, u32[]{:S(2)}) collective-permute-start(f32[616,128]{1,0:T(8,128)S(1)} %get-tuple-element.6.own), channel_id=1, source_target_pairs={{0,1},{1,0},{2,3},{3,2},{4,5},{5,4},{6,7},{7,6},{8,9},{9,8},{10,11... | collective-permute-start | bytes 946184 | tf_op jit(solution)/shard_map/ppermute | solution.py:386
  11.2 10.4 %collective-permute-start.3 = (f32[40,128]{1,0:T(8,128)S(1)}, f32[40,128]{1,0:T(8,128)S(1)}, u32[]{:S(2)}, u32[]{:S(2)}) collective-permute-start(f32[40,128]{1,0:T(8,128)S(1)} %get-tuple-element.7), channel_id=1, source_target_pairs={{0,504},{1,505},{2,506},{3,507},{4,508},{5,509},{6,510},{7,511},{8... | collective-permute-start | bytes 61448 | tf_op jit(solution)/shard_map/ppermute | solution.py:385
  19.7 5.7 %collective-permute-start.2 = (f32[40,128]{1,0:T(8,128)S(1)}, f32[40,128]{1,0:T(8,128)S(1)}, u32[]{:S(2)}, u32[]{:S(2)}) collective-permute-start(f32[40,128]{1,0:T(8,128)S(1)} %get-tuple-element.7), channel_id=1, source_target_pairs={{0,8},{1,9},{2,10},{3,11},{4,12},{5,13},{6,14},{7,15},{8,0},{9,1},... | collective-permute-start | bytes 61448 | tf_op jit(solution)/shard_map/ppermute | solution.py:384

commit v2 on v1

--- a/solution.py
+++ b/solution.py
@@ -87,7 +87,7 @@
 
 
 def step_kernel(
-    sz, own, pair_a, pair_b, col_e, col_w, out_t, out_s, out_u, out_v,
+    sz, own, col_e, col_w, pair_a, pair_b, out_t, out_s, out_u, out_v,
     south, north, star, coef, value, gain, outs, sems,
 ):
     levels = sz.levels
@@ -102,9 +102,9 @@
     def swap_rows(x):
         return jnp.where(even_row, pltpu.roll(x, 7, 0), pltpu.roll(x, 1, 0))
 
-    def fill(ref, source):
+    def fill(ref, source, start=0):
         for at in range(0, sz.total, 8):
-            ref[at : at + 8, :] = source[at : at + 8, :]
+            ref[at : at + 8, :] = source[start + at : start + at + 8, :]
 
     @pl.when(odd_lat)
     def _():
@@ -113,7 +113,7 @@
     @pl.when(jnp.logical_not(odd_lat))
     def _():
         fill(south, pair_b)
-        fill(north, pair_a)
+        fill(north, pair_a, sz.total)
 
     @pl.when(odd_lat & jnp.logical_not(on_top))
     def _():
@@ -383,7 +383,8 @@
     from_b = lax.ppermute(rows, names, pair_b)
     from_1 = lax.ppermute(cols, names, lon_1)
     from_2 = lax.ppermute(cols, names, lon_2)
-    from_a = lax.ppermute(rows, names, pair_a)
+    groups = [[i, j] for i, j in pair_a if i < j]
+    from_a = lax.all_gather(rows, names, axis_index_groups=groups, tiled=True)
     field = jax.ShapeDtypeStruct(temp.shape, f32)
     tall = 8 * 4 * sz.chunks
     return pl.pallas_call(
@@ -403,7 +404,7 @@
         ],
         compiler_params=pltpu.CompilerParams(vmem_limit_bytes=VMEM_LIMIT),
         name="step",
-    )(rows, from_a, from_b, from_1, from_2)
+    )(rows, from_1, from_2, from_a, from_b)
 
 
 def solution(mesh):

time: 27.5 us -> 24.8 us (0.902)
  the two profiles are of different devices: /device:TPU:128 before, /device:TPU:1 now
where the time goes in v2:
time: 24.8 us; the launch traced here: 24.6 us
  starting transfers between devices  18.2 us (73%)
  Pallas kernels  3.11 us (13%)
  blocking collectives  2.26 us (9%)
  between operations  0.67 us (3%)
  waiting for transfers between devices  0.34 us (1%)
    ppermute x1, starting transfers between devices, shards(): from_2 = lax.ppermute(cols, names, lon_2)  9.1 us
    ppermute x1, starting transfers between devices, shards(): from_b = lax.ppermute(rows, names, pair_b)  7.2 us
    all_gather x1, blocking collectives, shards(): from_a = lax.all_gather(rows, names, axis_index_groups=groups, tiled=True)  2.26 us
    ppermute x1, starting transfers between devices, shards(): from_1 = lax.ppermute(cols, names, lon_1)  1.92 us
    pallas_call x1, Pallas kernels, shards(): pl.pallas_call(functools.partial(step_kernel, sz), out_shape=(field,) * 4...  1.91 us
    pallas_call x1, Pallas kernels, shards(): pl.pallas_call(functools.partial(pack_kernel, sz), out_shape=(pltpu.VMEM(...  1.2 us
  transfers between devices with their start and end apart: 3, of which 1 were waited for; matrix products, arithmetic and copies ran while one was open for 0% of the time, Pallas kernels for 0%

profile of v2, /device:TPU:1, one launch (start us, length us, event | category | flops | bytes accessed | tf_op | source)
XLA Modules:
  0.0 24.6 jit_solution(9859335287106614288)
XLA Ops:
  0.6 1.2 %pack.1 = (f32[616,128]{1,0:T(8,128)S(1)}, f32[40,128]{1,0:T(8,128)S(1)}) custom-call(f32[75,2,128]{2,1,0:T(2,128)} %temp.1, f32[75,2,128]{2,1,0:T(2,128)} %salt.1, f32[75,2,128]{2,1,0:T(2,128)} %uvel.1, f32[75,2,128]{2,1,0:T(2,128)} %vvel.1, s32[2,128]{1,0:T(2,128)} %mask.1, s32[2,128]{1,0:T(2,128)} %bottom.1), custom_call_target="tpu_custom_call" | custom-call | tf_op jit(solution)/shard_map/pack/pallas_call | solution.py:367
  1.8 7.2 %collective-permute-start.2 = (f32[616,128]{1,0:T(8,128)S(1)}, f32[616,128]{1,0:T(8,128)S(1)}, u32[]{:S(2)}, u32[]{:S(2)}) collective-permute-start(f32[616,128]{1,0:T(8,128)S(1)} %get-tuple-element.6.own), channel_id=1, source_target_pairs={{1,2},{2,1},{3,4},{4,3},{5,6},{6,5},{7,511},{9,10},{10,9},{11,12},... | collective-permute-start | bytes 946184 | tf_op jit(solution)/shard_map/ppermute | solution.py:383
  9.0 9.1 %collective-permute-start.1 = (f32[40,128]{1,0:T(8,128)S(1)}, f32[40,128]{1,0:T(8,128)S(1)}, u32[]{:S(2)}, u32[]{:S(2)}) collective-permute-start(f32[40,128]{1,0:T(8,128)S(1)} %get-tuple-element.7), channel_id=1, source_target_pairs={{0,504},{1,505},{2,506},{3,507},{4,508},{5,509},{6,510},{7,511},{8... | collective-permute-start | bytes 61448 | tf_op jit(solution)/shard_map/ppermute | solution.py:385
  18.2 1.9 %collective-permute-start = (f32[40,128]{1,0:T(8,128)S(1)}, f32[40,128]{1,0:T(8,128)S(1)}, u32[]{:S(2)}, u32[]{:S(2)}) collective-permute-start(f32[40,128]{1,0:T(8,128)S(1)} %get-tuple-element.7), channel_id=1, source_target_pairs={{0,8},{1,9},{2,10},{3,11},{4,12},{5,13},{6,14},{7,15},{8,0},{9,1},... | collective-permute-start | bytes 61448 | tf_op jit(solution)/shard_map/ppermute | solution.py:384
  20.1 2.3 %all_gather.3.pair_a = f32[1232,128]{1,0:T(8,128)S(1)} all-gather(f32[616,128]{1,0:T(8,128)S(1)} %get-tuple-element.6.own), channel_id=1, replica_groups={{0,1},{2,3},{4,5},{6,7},{8,9},{10,11},{12,13},{14,15},{16,17},{18,19},{..., dimensions={0}, use_global_device_ids=true | all-gather | bytes 946176 | tf_op jit(solution)/shard_map/all_gather | solution.py:387
  22.3 0.0 collective-permute-done.1.col_w
  22.3 0.3 %collective-permute-done.col_e = f32[40,128]{1,0:T(8,128)S(1)} collective-permute-done((f32[40,128]{1,0:T(8,128)S(1)}, f32[40,128]{1,0:T(8,128)S(1)}, u32[]{:S(2)}, u32[]{:S(2)}) %collective-permute-start) | collective-permute-done | bytes 20512 | tf_op jit(solution)/shard_map/ppermute | solution.py:384
  22.7 0.0 collective-permute-done.2.pair_b
  22.7 1.9 %step.1 = (f32[75,2,128]{2,1,0:T(2,128)}, f32[75,2,128]{2,1,0:T(2,128)}, f32[75,2,128]{2,1,0:T(2,128)}, f32[75,2,128]{2,1,0:T(2,128)}) custom-call(f32[616,128]{1,0:T(8,128)S(1)} %get-tuple-element.6.own, f32[40,128]{1,0:T(8,128)S(1)} %collective-permute-done.col_e, f32[40,128]{1,0:T(8,128)S(1)} %collective-permute-done.1.col_w, ...), custom_call_target="tpu_custom_call" | custom-call | tf_op jit(solution)/shard_map/step/pallas_call | solution.py:390
Async XLA Ops:
  1.8 20.8 %collective-permute-start.2 = (f32[616,128]{1,0:T(8,128)S(1)}, f32[616,128]{1,0:T(8,128)S(1)}, u32[]{:S(2)}, u32[]{:S(2)}) collective-permute-start(f32[616,128]{1,0:T(8,128)S(1)} %get-tuple-element.6.own), channel_id=1, source_target_pairs={{1,2},{2,1},{3,4},{4,3},{5,6},{6,5},{7,511},{9,10},{10,9},{11,12},... | collective-permute-start | bytes 946184 | tf_op jit(solution)/shard_map/ppermute | solution.py:383
  9.0 13.3 %collective-permute-start.1 = (f32[40,128]{1,0:T(8,128)S(1)}, f32[40,128]{1,0:T(8,128)S(1)}, u32[]{:S(2)}, u32[]{:S(2)}) collective-permute-start(f32[40,128]{1,0:T(8,128)S(1)} %get-tuple-element.7), channel_id=1, source_target_pairs={{0,504},{1,505},{2,506},{3,507},{4,508},{5,509},{6,510},{7,511},{8... | collective-permute-start | bytes 61448 | tf_op jit(solution)/shard_map/ppermute | solution.py:385
  18.2 4.5 %collective-permute-start = (f32[40,128]{1,0:T(8,128)S(1)}, f32[40,128]{1,0:T(8,128)S(1)}, u32[]{:S(2)}, u32[]{:S(2)}) collective-permute-start(f32[40,128]{1,0:T(8,128)S(1)} %get-tuple-element.7), channel_id=1, source_target_pairs={{0,8},{1,9},{2,10},{3,11},{4,12},{5,13},{6,14},{7,15},{8,0},{9,1},... | collective-permute-start | bytes 61448 | tf_op jit(solution)/shard_map/ppermute | solution.py:384

commit v3 on v2

--- a/solution.py
+++ b/solution.py
@@ -251,26 +251,26 @@
     middle = (levels + 1) // 2
     one = jnp.ones((8, LANES), jnp.float32)
     a_next = at(coef, 0)
-    theta, phi, y = one, zero, zero
-    theta_b, phi_b, y_b = one, zero, zero
+    theta, before, y = one, zero, zero
+    theta_b, before_b, y_b = one, zero, zero
     b_next = zero
     for i in range(middle):
         k = i
         a_k, a_next = a_next, at(coef, k + 1)
-        phi = theta + a_k * phi
-        theta_new = phi + a_next * theta
+        theta_new = (1.0 + a_k + a_next) * theta - (a_k * a_k) * before
+        before = theta
         inverse = theta * pl.reciprocal(theta_new, approx=False)
-        y = inverse * (at(star, k) + a_k * y)
+        y = inverse * at(star, k) + (inverse * a_k) * y
         value[8 * k : 8 * k + 8, :] = y
         gain[8 * k : 8 * k + 8, :] = a_next * inverse
         theta = theta_new
         k = levels - 1 - i
         if k >= middle:
             b_k, b_next = b_next, at(coef, k)
-            phi_b = theta_b + b_k * phi_b
-            theta_new = phi_b + b_next * theta_b
+            theta_new = (1.0 + b_k + b_next) * theta_b - (b_k * b_k) * before_b
+            before_b = theta_b
             inverse = theta_b * pl.reciprocal(theta_new, approx=False)
-            y_b = inverse * (at(star, k) + b_k * y_b)
+            y_b = inverse * at(star, k) + (inverse * b_k) * y_b
             value[8 * k : 8 * k + 8, :] = y_b
             gain[8 * k : 8 * k + 8, :] = b_next * inverse
             theta_b = theta_new

time: 24.8 us -> 24.9 us (level)
  no operation moved by 1% of the time
where the time goes in v3:
time: 24.9 us; the launch traced here: 24.6 us
  starting transfers between devices  18.2 us (73%)
  Pallas kernels  3.15 us (13%)
  blocking collectives  2.26 us (9%)
  between operations  0.67 us (3%)
  waiting for transfers between devices  0.34 us (1%)
    ppermute x1, starting transfers between devices, shards(): from_2 = lax.ppermute(cols, names, lon_2)  9.1 us
    ppermute x1, starting transfers between devices, shards(): from_b = lax.ppermute(rows, names, pair_b)  7.2 us
    all_gather x1, blocking collectives, shards(): from_a = lax.all_gather(rows, names, axis_index_groups=groups, tiled=True)  2.26 us
    pallas_call x1, Pallas kernels, shards(): pl.pallas_call(functools.partial(step_kernel, sz), out_shape=(field,) * 4...  1.95 us
    ppermute x1, starting transfers between devices, shards(): from_1 = lax.ppermute(cols, names, lon_1)  1.92 us
    pallas_call x1, Pallas kernels, shards(): pl.pallas_call(functools.partial(pack_kernel, sz), out_shape=(pltpu.VMEM(...  1.2 us
  transfers between devices with their start and end apart: 3, of which 1 were waited for; matrix products, arithmetic and copies ran while one was open for 0% of the time, Pallas kernels for 0%

profile of v3, /device:TPU:1, one launch (start us, length us, event | category | flops | bytes accessed | tf_op | source)
XLA Modules:
  0.0 24.6 jit_solution(16580931254443810009)
XLA Ops:
  0.6 1.2 %pack.1 = (f32[616,128]{1,0:T(8,128)S(1)}, f32[40,128]{1,0:T(8,128)S(1)}) custom-call(f32[75,2,128]{2,1,0:T(2,128)} %temp.1, f32[75,2,128]{2,1,0:T(2,128)} %salt.1, f32[75,2,128]{2,1,0:T(2,128)} %uvel.1, f32[75,2,128]{2,1,0:T(2,128)} %vvel.1, s32[2,128]{1,0:T(2,128)} %mask.1, s32[2,128]{1,0:T(2,128)} %bottom.1), custom_call_target="tpu_custom_call" | custom-call | tf_op jit(solution)/shard_map/pack/pallas_call | solution.py:367
  1.8 7.2 %collective-permute-start.2 = (f32[616,128]{1,0:T(8,128)S(1)}, f32[616,128]{1,0:T(8,128)S(1)}, u32[]{:S(2)}, u32[]{:S(2)}) collective-permute-start(f32[616,128]{1,0:T(8,128)S(1)} %get-tuple-element.6.own), channel_id=1, source_target_pairs={{1,2},{2,1},{3,4},{4,3},{5,6},{6,5},{7,511},{9,10},{10,9},{11,12},... | collective-permute-start | bytes 946184 | tf_op jit(solution)/shard_map/ppermute | solution.py:383
  9.0 9.1 %collective-permute-start.1 = (f32[40,128]{1,0:T(8,128)S(1)}, f32[40,128]{1,0:T(8,128)S(1)}, u32[]{:S(2)}, u32[]{:S(2)}) collective-permute-start(f32[40,128]{1,0:T(8,128)S(1)} %get-tuple-element.7), channel_id=1, source_target_pairs={{0,504},{1,505},{2,506},{3,507},{4,508},{5,509},{6,510},{7,511},{8... | collective-permute-start | bytes 61448 | tf_op jit(solution)/shard_map/ppermute | solution.py:385
  18.2 1.9 %collective-permute-start = (f32[40,128]{1,0:T(8,128)S(1)}, f32[40,128]{1,0:T(8,128)S(1)}, u32[]{:S(2)}, u32[]{:S(2)}) collective-permute-start(f32[40,128]{1,0:T(8,128)S(1)} %get-tuple-element.7), channel_id=1, source_target_pairs={{0,8},{1,9},{2,10},{3,11},{4,12},{5,13},{6,14},{7,15},{8,0},{9,1},... | collective-permute-start | bytes 61448 | tf_op jit(solution)/shard_map/ppermute | solution.py:384
  20.1 2.3 %all_gather.3.pair_a = f32[1232,128]{1,0:T(8,128)S(1)} all-gather(f32[616,128]{1,0:T(8,128)S(1)} %get-tuple-element.6.own), channel_id=1, replica_groups={{0,1},{2,3},{4,5},{6,7},{8,9},{10,11},{12,13},{14,15},{16,17},{18,19},{..., dimensions={0}, use_global_device_ids=true | all-gather | bytes 946176 | tf_op jit(solution)/shard_map/all_gather | solution.py:387
  22.3 0.0 collective-permute-done.1.col_w
  22.3 0.3 %collective-permute-done.col_e = f32[40,128]{1,0:T(8,128)S(1)} collective-permute-done((f32[40,128]{1,0:T(8,128)S(1)}, f32[40,128]{1,0:T(8,128)S(1)}, u32[]{:S(2)}, u32[]{:S(2)}) %collective-permute-start) | collective-permute-done | bytes 20512 | tf_op jit(solution)/shard_map/ppermute | solution.py:384
  22.7 0.0 collective-permute-done.2.pair_b
  22.7 2.0 %step.1 = (f32[75,2,128]{2,1,0:T(2,128)}, f32[75,2,128]{2,1,0:T(2,128)}, f32[75,2,128]{2,1,0:T(2,128)}, f32[75,2,128]{2,1,0:T(2,128)}) custom-call(f32[616,128]{1,0:T(8,128)S(1)} %get-tuple-element.6.own, f32[40,128]{1,0:T(8,128)S(1)} %collective-permute-done.col_e, f32[40,128]{1,0:T(8,128)S(1)} %collective-permute-done.1.col_w, ...), custom_call_target="tpu_custom_call" | custom-call | tf_op jit(solution)/shard_map/step/pallas_call | solution.py:390
Async XLA Ops:
  1.8 20.8 %collective-permute-start.2 = (f32[616,128]{1,0:T(8,128)S(1)}, f32[616,128]{1,0:T(8,128)S(1)}, u32[]{:S(2)}, u32[]{:S(2)}) collective-permute-start(f32[616,128]{1,0:T(8,128)S(1)} %get-tuple-element.6.own), channel_id=1, source_target_pairs={{1,2},{2,1},{3,4},{4,3},{5,6},{6,5},{7,511},{9,10},{10,9},{11,12},... | collective-permute-start | bytes 946184 | tf_op jit(solution)/shard_map/ppermute | solution.py:383
  9.0 13.3 %collective-permute-start.1 = (f32[40,128]{1,0:T(8,128)S(1)}, f32[40,128]{1,0:T(8,128)S(1)}, u32[]{:S(2)}, u32[]{:S(2)}) collective-permute-start(f32[40,128]{1,0:T(8,128)S(1)} %get-tuple-element.7), channel_id=1, source_target_pairs={{0,504},{1,505},{2,506},{3,507},{4,508},{5,509},{6,510},{7,511},{8... | collective-permute-start | bytes 61448 | tf_op jit(solution)/shard_map/ppermute | solution.py:385
  18.2 4.5 %collective-permute-start = (f32[40,128]{1,0:T(8,128)S(1)}, f32[40,128]{1,0:T(8,128)S(1)}, u32[]{:S(2)}, u32[]{:S(2)}) collective-permute-start(f32[40,128]{1,0:T(8,128)S(1)} %get-tuple-element.7), channel_id=1, source_target_pairs={{0,8},{1,9},{2,10},{3,11},{4,12},{5,13},{6,14},{7,15},{8,0},{9,1},... | collective-permute-start | bytes 61448 | tf_op jit(solution)/shard_map/ppermute | solution.py:384
